TPU v7x, 512 devices: a whole 4x8x8 slice. The times are simulated.
512 devices in a mesh: wide: 64 (over z_lo, y, core), narrow: 8 (over x, z_hi).
Axes of the slice: x: 4, y: 8, z: 8 (z_hi: 2, z_lo: 4; z = z_hi * 4 + z_lo), core: 2. Of those that a mesh axis runs over, the one named last changes fastest.
Arguments:
- grad: bfloat16 [4096, 16384], P('wide', 'narrow'), may hold values from -6 to 6
- left_codes: int32 [4096, 4096], P('wide', 'narrow'), may hold values from -8 to 7
- left_scales: int32 [4096, 32], P('wide', 'narrow'), may hold values from 2 to 6
- left_error: bfloat16 [4096, 4096], P('wide', 'narrow'), may hold values from -0.0029907227 to 0.0029907227
- right_codes: int32 [16, 1024, 1024], P('narrow', 'wide'), may hold values from -8 to 7
- right_scales: int32 [16, 1024, 8], P('narrow', 'wide'), may hold values from 3 to 7
- right_error: bfloat16 [16, 1024, 1024], P('narrow', 'wide'), may hold values from -0.0059814453 to 0.0059814453
- first_moment: float32 [8, 2048, 4096], P(None, 'wide', 'narrow'), may hold values from -6 to 6
- second_moment: float32 [8, 2048, 4096], P(None, 'wide', 'narrow'), may hold values from 0.5 to 4
Outputs:
- update: bfloat16 [4096, 16384], P('wide', 'narrow')
- new_first: float32 [8, 2048, 4096], P(None, 'wide', 'narrow')
- new_second: float32 [8, 2048, 4096], P(None, 'wide', 'narrow')
All inputs are finite; a program needn't handle non-finite values.
Results may differ from a plain program's by a relative error of at most 0.007.
Values may be sent and summed in bfloat16 or wider, within the bound.
A program may use at most 64 MiB of HBM per device.

v0:
```python
import functools
import math

import jax
import jax.numpy as jnp
from jax import lax
from jax.experimental import pallas as pl
from jax.experimental.pallas import tpu as pltpu
from jax.sharding import PartitionSpec as P

MESH = pl.DeviceIdType.MESH
F32, BF16 = jnp.float32, jnp.bfloat16
BETA_ONE = 0.95
BETA_TWO = 0.95
EPSILON = 1e-08
NX = 4
NH = 2


def dequantized(codes, scales, error, quantum):
    groups, columns = scales.shape[0], codes.shape[1]
    column = lax.broadcasted_iota(jnp.int32, (groups, columns), 1) // (columns // groups)
    spread = (column == lax.broadcasted_iota(jnp.int32, (groups, columns), 0)).astype(F32).astype(BF16)
    expanded = lax.dot_general(
        scales.astype(F32).astype(BF16), spread, (((0,), (0,)), ((), ())), preferred_element_type=F32
    )
    return (codes.astype(F32) * expanded * quantum + error.astype(F32)).astype(BF16)


def kernel(nz, ny, *refs):
    inputs, refs = refs[:9], refs[9:]
    outputs, fetched, held, refs = refs[:3], refs[3:12], refs[12:15], refs[15:]
    update, new_first, new_second = held
    grad, lcodes, lscales, lerror, rcodes, rscales, rerror, first, second = fetched
    (
        turned,
        right,
        left,
        rstage,
        lstage,
        outgoing,
        slabs,
        total,
        direction,
        partial,
        halfway,
        arrived,
        home,
        back,
        result,
        foreign,
    ) = refs[:16]
    (
        fetch_sem,
        sib_s,
        sib_r,
        grad_s,
        grad_r,
        zr_s,
        zr_r,
        zl_s,
        zl_r,
        za_s,
        za_r,
        zb_s,
        zb_r,
        yr_s,
        yr_r,
        late_s,
        late_r,
        ya_s,
        ya_r,
        yb_s,
        yb_r,
        share_s,
        share_r,
        out_s,
        out_r,
        back_s,
        back_r,
        own_sem,
        ring_s,
        ring_r,
        sum_s,
        sum_r,
    ) = refs[16:]
    nq = nz * ny
    block = 32 * nq
    order = 128 * nq
    span = lcodes.shape[1]
    half = span // 2
    hb = block // 2
    wide, narrow = lax.axis_index("wide"), lax.axis_index("narrow")
    core, chip = lax.rem(wide, 2), wide // 2
    z, y = chip // ny, lax.rem(chip, ny)
    x, high = narrow // NH, lax.rem(narrow, NH)
    other = 1 - core
    pair, odd = z // 2, lax.rem(z, 2)
    place = (pair * ny + y) * 2 + odd
    side = wide // nq
    has_own = side == core
    sends_own = wide // (nq // 2) == 2 * core + odd

    fetches = [pltpu.make_async_copy(a, b, fetch_sem.at[i]) for i, (a, b) in enumerate(zip(inputs, fetched))]
    for i in (4, 5, 6, 1, 2, 3, 0, 7, 8):
        fetches[i].start()

    def wide_at(zz, yy, cc):
        return (zz * ny + yy) * 2 + cc

    def copy(src, dst, send, recv, ww, nn):
        return pltpu.make_async_remote_copy(
            src_ref=src, dst_ref=dst, send_sem=send, recv_sem=recv, device_id=(ww, nn), device_id_type=MESH
        )

    def start(copies):
        for c in copies:
            c.start()

    def landed(copies):
        for c in copies:
            c.wait_recv()

    sibling = wide + 1 - 2 * core
    y_up, y_down = lax.rem(y + 1, ny), lax.rem(y + ny - 1, ny)
    x_up, x_down = lax.rem(x + 1, NX), lax.rem(x + NX - 1, NX)
    x_far = lax.rem(x + 2, NX)
    n_up, n_down = x_up * NH + high, x_down * NH + high
    w_up, w_down = wide_at(z, y_up, core), wide_at(z, y_down, core)

    barrier = pltpu.get_barrier_semaphore()
    plane = 2 * nq * NH

    for extra in range(NH):
        nn = x * NH + lax.rem(high + extra, NH)

        def greet(i, carry):
            there = wide + i
            there = jnp.where(there >= 2 * nq, there - 2 * nq, there)
            pl.semaphore_signal(barrier, inc=1, device_id=(there, nn), device_id_type=MESH)
            return carry

        lax.fori_loop(1 if extra == 0 else 0, 2 * nq, greet, 0)
    for nn in (n_up, n_down):
        pl.semaphore_signal(barrier, inc=1, device_id=(wide, nn), device_id_type=MESH)

    rows16 = pl.ds(pl.multiple_of(core * 16, 16), 16)
    rows64 = pl.ds(pl.multiple_of(core * 64, 64), 64)
    quantum = 1.0 / (16.0 * math.sqrt(block))
    for i in (4, 5, 6):
        fetches[i].wait()
    for ref, which in ((rstage, other), (right.at[:, z, y, rows16, :], core)):
        value = dequantized(rcodes[which], rscales[which], rerror[which], quantum)
        for h in range(2):
            ref[h] = value[:, h * hb : (h + 1) * hb]
    pl.semaphore_wait(barrier, plane - 1 + 2)
    sib = [
        copy(rstage, right.at[:, z, y, rows16, :], sib_s.at[0], sib_r.at[0], sibling, narrow),
        copy(lstage, left.at[other, pair, y, odd, rows64, :], sib_s.at[1], sib_r.at[1], sibling, narrow),
    ]
    rows_g = pl.ds(pl.multiple_of(odd * 128 + core * 64, 64), 64)
    beside = wide_at(z + 1 - 2 * odd, y, core)
    own_block = grad.at[:, pl.ds(pl.multiple_of(core * block, block), block)]
    other_block = grad.at[:, pl.ds(pl.multiple_of(other * block, block), block)]
    rows_out = [
        copy(other_block, turned.at[rows_g, :], grad_s.at[0], grad_r.at[0], sibling, narrow),
        copy(own_block, turned.at[rows_g, :], grad_s.at[1], grad_r.at[1], beside, narrow),
        copy(other_block, turned.at[rows_g, :], grad_s.at[2], grad_r.at[2], beside + 1 - 2 * core, narrow),
    ]
    sib[0].start()
    quantum = 1.0 / (16.0 * math.sqrt(order))
    for i in (1, 2, 3):
        fetches[i].wait()
    value = dequantized(lcodes[...], lscales[...], lerror[...], quantum)
    for h in range(2):

        @pl.when(core == h)
        def _():
            left[h, pair, y, odd, rows64, :] = value[:, h * half : (h + 1) * half]

        @pl.when(core != h)
        def _():
            lstage[...] = value[:, h * half : (h + 1) * half]

    sib[1].start()

    last = ny // 2

    def along_z(ref_for, send, recv):
        made = []
        for d in range(1, nz):
            ref = ref_for(lax.rem(z + d, nz))
            made.append(copy(ref, ref, send.at[d - 1], recv.at[d - 1], wide_at(lax.rem(z + d, nz), y, core), narrow))
        return made

    def passed(t):
        return lax.rem(y + ny - (t - 1), ny), lax.rem(y + (t - 1), ny)

    nearest = [0, 1, nz - 1][: min(nz, 3)] + list(range(2, nz - 1))
    if nz == 2:
        nearest = [0, 1]
    zr = along_z(lambda zz: right.at[lax.rem(zz, 2), z, y], zr_s, zr_r)
    zlate = along_z(lambda zz: right.at[1 - lax.rem(zz, 2), z, y], zl_s, zl_r)

    def ring_right(t, e):
        zz = lax.rem(z + nz - e, nz)
        at = nearest.index(e)
        made = []
        for way, (yy, ww) in enumerate(zip(passed(t), (w_up, w_down))):
            if t < last or (at < nz // 2) == (way == 0):
                ref = right.at[odd, zz, yy]
                made.append(copy(ref, ref, yr_s.at[t - 1, e, way], yr_r.at[t - 1, e, way], ww, narrow))
        return made

    yr = [[ring_right(t, e) for e in nearest] for t in range(1, last + 1)]

    ra = 96
    rb = 128 - ra

    def rows_a(yy, zs=slice(None)):
        return left.at[core, :, yy, zs, pl.ds(0, ra)]

    def rows_b(yy, begin=0, size=rb):
        return left.at[core, pair, yy, odd, pl.ds(ra + begin, size)]

    own_a = left.at[core, pair, y, odd, pl.ds(0, ra)]
    za = along_z(lambda zz: own_a, za_s, za_r)
    zb = along_z(lambda zz: rows_b(pl.ds(0, ny)), zb_s, zb_r)
    ya, yb, late = [], [], []

    def both_ways(t, a, b, send, recv):
        return [
            copy(a, a, send.at[t - 1, 0], recv.at[t - 1, 0], w_up, narrow),
            copy(b, b, send.at[t - 1, 1], recv.at[t - 1, 1], w_down, narrow),
        ]

    for t in range(1, last + 1):
        up, down = passed(t)
        if t < last:
            a, b = rows_a(up), rows_a(down)
        else:
            a, b = rows_a(up, pl.ds(0, 1)), rows_a(down, pl.ds(1, 1))
        ya.append(both_ways(t, a, b, ya_s, ya_r))
        a, b = (rows_b(up), rows_b(down)) if t < last else (rows_b(up, 0, rb // 2), rows_b(down, rb // 2, rb // 2))
        yb.append(both_ways(t, a, b, yb_s, yb_r))
        zs = (pl.ds(0, nz), pl.ds(0, nz)) if t < last else (pl.ds(0, nz // 2), pl.ds(nz // 2, nz // 2))
        a, b = right.at[1 - odd, zs[0], up], right.at[1 - odd, zs[1], down]
        late.append(both_ways(t, a, b, late_s, late_r))
    shares = []

    def share(ref):
        at = len(shares)
        c = copy(ref, ref, share_s.at[at], share_r.at[at], sibling, narrow)
        c.start()
        shares.append(c)

    sib[0].wait_recv()
    start(yr[0][0])
    start(zr)
    fetches[0].wait()
    for h in range(2):

        @pl.when(core == h)
        def _():
            turned[rows_g, :] = grad[:, h * block : (h + 1) * block]

    start(rows_out)
    sib[1].wait_recv()
    start(yb[0])
    start(za)
    for at, e in enumerate(nearest):
        if at > 0:
            zr[e - 1].wait_recv()
            start(yr[0][at])
    start(zlate)
    b_step = 1

    def next_b(t):
        landed(yb[t - 1])
        if t < last:
            start(yb[t])
        else:
            start(zb)
            share(rows_b(pl.ds(0, ny)))

    for t in range(2, last + 1):
        for at in range(nz):
            landed(yr[t - 2][at])
            start(yr[t - 1][at])
            if at % 2 == 1 and b_step <= last and t < last:
                next_b(b_step)
                b_step += 1
    while b_step <= last:
        next_b(b_step)
        b_step += 1
    landed(za)
    share(rows_a(y))
    for at in range(nz):
        landed(yr[last - 1][at])

    landed(rows_out)
    wide_n = min(256, hb)
    for at in range(0, hb, wide_n):
        basis = right[odd, :, :, :, at : at + wide_n].reshape(block, wide_n)
        value = jnp.dot(turned[...], basis, preferred_element_type=F32).T.astype(BF16)
        for d in range(2):
            outgoing[at // 32 : (at + wide_n) // 32, d] = value[:, d * 128 : (d + 1) * 128].reshape(wide_n // 32, 32, 128)

    lands = slabs.at[pl.ds(narrow * nq + place - odd, 2)]
    high_far = 1 - high
    n_far = x * NH + high_far
    first_to = (nq // 2) * (2 * core + odd)

    def send_near(t, carry):
        j = lax.rem(2 * y + pair + t, nq // 2)
        to = first_to + j

        @pl.when(to != wide)
        def _():
            copy(outgoing.at[j], lands, out_s.at[0], out_r.at[0], to, narrow).start()

        @pl.when(to == wide)
        def _():
            pltpu.make_async_copy(outgoing.at[j], lands, own_sem.at[0]).start()

        return carry

    def send_far(t, carry):
        j = lax.rem(2 * y + pair + t, nq // 2)
        copy(outgoing.at[j], lands, out_s.at[1], out_r.at[1], first_to + j, n_far).start()
        return carry

    lax.fori_loop(0, nq // 2, send_near, 0)
    lax.fori_loop(0, nq // 2, send_far, 0)
    start(ya[0])

    def wait_near(ref, base, send, recv, sending, some_own=has_own, own_many=1):
        def wait(many):
            there = ref.at[pl.ds(base, many)]
            c = copy(there, there, send, recv, sibling, narrow)
            if sending:
                c.wait_send()
            else:
                c.wait_recv()

        @pl.when(some_own)
        def _():
            wait(nq - own_many)

        @pl.when(jnp.logical_not(some_own))
        def _():
            wait(nq)

    def wait_far(ref, base, send, recv, sending):
        there = ref.at[pl.ds(base, nq)]
        c = copy(there, there, send, recv, sibling, narrow)
        if sending:
            c.wait_send()
        else:
            c.wait_recv()

    def next_a(t):
        landed(ya[t - 1])
        if t < last:
            start(ya[t])
            for yy in passed(t + 1):
                share(rows_a(yy))
        else:
            share(rows_a(lax.rem(y + last, ny)))

    hq = nq // 2

    def slab_at(xx, g):
        return (xx * NH + g) * nq

    def ring_x(g, at):
        own = slabs.at[pl.ds(slab_at(x, g), nq)]
        from_down = slabs.at[pl.ds(slab_at(x_down, g), hq)]
        from_up = slabs.at[pl.ds(slab_at(x_up, g) + hq, hq)]
        return [
            copy(own, own, ring_s.at[at, 0], ring_r.at[at, 0], wide, n_up),
            copy(own, own, ring_s.at[at, 1], ring_r.at[at, 1], wide, n_down),
            copy(from_down, from_down, ring_s.at[at, 2], ring_r.at[at, 2], wide, n_up),
            copy(from_up, from_up, ring_s.at[at, 3], ring_r.at[at, 3], wide, n_down),
        ]

    ring_near, ring_far = ring_x(high, 0), ring_x(high_far, 1)
    wait_near(slabs, slab_at(x, high), out_s.at[0], out_r.at[0], False, sends_own, 2)

    @pl.when(sends_own)
    def _():
        pltpu.make_async_copy(outgoing.at[0], lands, own_sem.at[0]).wait()

    start(ring_near[:2])
    for t in range(1, last + 1):
        next_a(t)
        if t == last - 2 or (last == 2 and t == 1):
            landed(ring_near[:2])
            start(ring_near[2:])
            wait_far(slabs, slab_at(x, high_far), out_s.at[1], out_r.at[1], False)
            start(ring_far[:2])
    landed(zlate)
    start(late[0])
    landed(zb)
    for d in range(1, nz):
        zz = lax.rem(z + nz - d, nz)
        share(left.at[core, zz // 2, pl.ds(0, ny), lax.rem(zz, 2), pl.ds(ra, rb)])
    landed(ring_far[:2])
    start(ring_far[2:])
    landed(ring_near[2:])
    landed(shares)
    landed(ring_far[2:])

    total[...] = jnp.zeros_like(total)
    deep = 4

    def rotate(i, carry):
        at = i * deep
        zz, yy = i // (2 * ny // deep), lax.rem(i, 2 * ny // deep) * (deep // 2)
        lhs = jnp.concatenate(
            [
                jnp.concatenate([slabs[s * nq + at + d] for s in range(NX * NH)], axis=0)
                for d in range(deep)
            ],
            axis=1,
        )
        for h in range(2):
            rhs = left[h, zz, pl.ds(yy, deep // 2)].reshape(deep * 128, half)
            total[:, h * half : (h + 1) * half] += jnp.dot(lhs, rhs, preferred_element_type=F32)
        return carry

    def next_late(t):
        landed(late[t - 1])
        if t < last:
            start(late[t])

    lax.fori_loop(0, nq // deep, rotate, 0)
    next_late(1)
    fetches[7].wait()
    fetches[8].wait()

    def moments(s, carry):
        there = pl.ds(pl.multiple_of(s * 32, 32), 32)
        value = total[there, :]
        m = BETA_ONE * first[s] + (1.0 - BETA_ONE) * value
        v = BETA_TWO * second[s] + (1.0 - BETA_TWO) * value * value
        new_first[s] = m
        new_second[s] = v
        direction[there, :] = (m / (jnp.sqrt(v) + EPSILON)).astype(BF16)
        return carry

    lax.fori_loop(0, NX * NH, moments, 0)
    stores = [pltpu.make_async_copy(held[i], outputs[i], fetch_sem.at[9 + i]) for i in range(3)]
    stores[1].start()
    stores[2].start()

    def rotate_back(i, carry):
        at = i * 2
        zz, yy = i // ny, lax.rem(i, ny)
        value = None
        for h in range(2):
            rhs = left[h, zz, yy].reshape(256, half)
            term = lax.dot_general(
                direction[:, h * half : (h + 1) * half],
                rhs,
                (((1,), (1,)), ((), ())),
                preferred_element_type=F32,
            )
            value = term if value is None else value + term
        value = value.astype(BF16)
        for s in range(NX * NH):
            for d in range(2):
                partial[s * nq + at + d] = value[s * 32 : (s + 1) * 32, d * 128 : (d + 1) * 128]
        return carry

    def sums_of(g, at):
        def part(xx, h):
            return partial.at[pl.ds(slab_at(xx, g) + h * hq, hq)]

        lower, upper = pl.ds(0, hq), pl.ds(hq, hq)
        made = [
            (part(x_far, 0), halfway.at[at, 0], n_up),
            (part(x_far, 1), halfway.at[at, 1], n_down),
            (part(x_down, 0), arrived.at[at, 1, lower], n_down),
            (part(x_up, 1), arrived.at[at, 0, upper], n_up),
            (part(x_up, 0), arrived.at[at, 0, lower], n_up),
            (part(x_down, 1), arrived.at[at, 1, upper], n_down),
        ]
        return [copy(a, b, sum_s.at[at, i], sum_r.at[at, i], wide, nn) for i, (a, b, nn) in enumerate(made)]

    sums_far, sums_near = sums_of(high_far, 0), sums_of(high, 1)
    few = min(8, hq)

    def pass_on(g, at):
        def some(i, carry):
            for h, base in ((0, slab_at(x_up, g)), (1, slab_at(x_down, g) + hq)):
                there = pl.ds(base + i * few, few)
                held = halfway[at, h, pl.ds(i * few, few)]
                partial[there] = (partial[there].astype(F32) + held.astype(F32)).astype(BF16)
            return carry

        lax.fori_loop(0, hq // few, some, 0)

    def add_up(g, at):
        def some(i, carry):
            there = pl.ds(i * few, few)
            value = partial[pl.ds(slab_at(x, g) + i * few, few)].astype(F32) + arrived[at, 0, there].astype(F32)
            home[pl.ds(at * nq + i * few, few)] = (value + arrived[at, 1, there].astype(F32)).astype(BF16)
            return carry

        lax.fori_loop(0, nq // few, some, 0)

    lax.fori_loop(0, nq // 4, rotate_back, 0)
    start((sums_far[0], sums_far[2]))
    lax.fori_loop(nq // 4, nq // 2, rotate_back, 0)
    next_late(2)
    start((sums_far[1], sums_far[3]))
    start(sums_near[:2])
    landed(sums_far[:2])
    pass_on(high_far, 0)
    start(sums_far[4:])
    start(sums_near[2:4])
    landed(sums_near[:2])
    pass_on(high, 1)
    start(sums_near[4:])
    for t in range(3, last + 1):
        next_late(t)

    goes_to = high * nq + lax.rem(wide, nq)

    def owner(at):
        zz, yy = at // (2 * ny) * 2 + lax.rem(at, 2), lax.rem(at // 2, ny)
        return wide_at(zz, yy, side)

    def back_far(t, carry):
        at = lax.rem(place + t, nq)
        copy(home.at[at], back.at[goes_to], back_s.at[1], back_r.at[1], owner(at), n_far).start()
        return carry

    def back_near(t, carry):
        at = lax.rem(place + t, nq)
        to = owner(at)
        src = home.at[nq + at]

        @pl.when(to != wide)
        def _():
            copy(src, back.at[goes_to], back_s.at[0], back_r.at[0], to, narrow).start()

        @pl.when(to == wide)
        def _():
            pltpu.make_async_copy(src, back.at[goes_to], own_sem.at[1]).start()

        return carry

    landed(sums_far[2:])
    add_up(high_far, 0)
    lax.fori_loop(0, nq, back_far, 0)
    landed(sums_near[2:])
    add_up(high, 1)
    lax.fori_loop(0, nq, back_near, 0)
    wait_far(back, high_far * nq, back_s.at[1], back_r.at[1], False)
    wait_near(back, high * nq, back_s.at[0], back_r.at[0], False)

    @pl.when(has_own)
    def _():
        pltpu.make_async_copy(home.at[0], back.at[goes_to], own_sem.at[1]).wait()

    turned_back = (back[0:nq].astype(F32) + back[nq : 2 * nq].astype(F32)).astype(BF16).reshape(block, 128)
    tall = ny * 32
    for zz in range(nz):
        value = sum(
            jnp.dot(
                right[h, zz].reshape(tall, hb), turned_back[h * hb : (h + 1) * hb], preferred_element_type=F32
            )
            for h in range(2)
        )
        value = value.T.astype(BF16)
        result[0, :, zz * tall : (zz + 1) * tall] = value[0:64]
        result[1, :, zz * tall : (zz + 1) * tall] = value[64:128]
    swap = copy(result.at[other], foreign, sib_s.at[3], sib_r.at[3], sibling, narrow)
    swap.start()
    for h in range(2):

        @pl.when(core == h)
        def _():
            update[:, h * block : (h + 1) * block] = result[core]

    swap.wait_recv()
    for h in range(2):

        @pl.when(core != h)
        def _():
            update[:, h * block : (h + 1) * block] = foreign[...]

    stores[0].start()

    sent = sib + rows_out + zr + zlate + za + zb + [c for step in yr for part in step for c in part]
    sent += [c for part in ya + yb + late for c in part] + shares + ring_near + ring_far + sums_near + sums_far + [swap]
    for c in sent:
        c.wait_send()
    for c in stores:
        c.wait()
    wait_near(slabs, slab_at(x, high), out_s.at[0], out_r.at[0], True, sends_own, 2)
    wait_far(slabs, slab_at(x, high_far), out_s.at[1], out_r.at[1], True)
    wait_near(back, high * nq, back_s.at[0], back_r.at[0], True)
    wait_far(back, high_far * nq, back_s.at[1], back_r.at[1], True)


def solution(mesh):
    nz, ny = 4, mesh.shape["wide"] // 8

    def step(*args):
        return body(nz, ny, *args)

    placed = (
        P("wide", "narrow"),
        P("wide", "narrow"),
        P("wide", "narrow"),
        P("wide", "narrow"),
        P("narrow", "wide", None),
        P("narrow", "wide", None),
        P("narrow", "wide", None),
        P(None, "wide", "narrow"),
        P(None, "wide", "narrow"),
    )
    return jax.shard_map(
        step,
        mesh=mesh,
        in_specs=placed,
        out_specs=(P("wide", "narrow"), P(None, "wide", "narrow"), P(None, "wide", "narrow")),
        check_vma=False,
    )


def body(nz, ny, *args):
    nq = nz * ny
    block, span = 32 * nq, args[1].shape[1]
    half = span // 2
    slabs = NX * NH
    dma = pltpu.SemaphoreType.DMA
    steps = ny // 2
    anywhere = pl.BlockSpec(memory_space=pl.ANY)
    args = list(args)
    args[2] = args[2].T
    args[5] = jnp.swapaxes(args[5], 1, 2)
    return pl.pallas_call(
        functools.partial(kernel, nz, ny),
        out_shape=(
            jax.ShapeDtypeStruct(args[0].shape, BF16),
            jax.ShapeDtypeStruct(args[7].shape, F32),
            jax.ShapeDtypeStruct(args[8].shape, F32),
        ),
        in_specs=[anywhere] * 9,
        out_specs=(anywhere,) * 3,
        scratch_shapes=[pltpu.VMEM(a.shape, a.dtype) for a in args + [args[0], args[7], args[8]]]
        + [
            pltpu.VMEM((256, block), BF16),
            pltpu.VMEM((2, nz, ny, 32, block // 2), BF16),
            pltpu.VMEM((2, nz // 2, ny, 2, 128, half), BF16),
            pltpu.VMEM((2, 16, block // 2), BF16),
            pltpu.VMEM((64, half), BF16),
            pltpu.VMEM((nq // 2, 2, 32, 128), BF16),
            pltpu.VMEM((slabs * nq, 32, 128), BF16),
            pltpu.VMEM((slabs * 32, span), F32),
            pltpu.VMEM((slabs * 32, span), BF16),
            pltpu.VMEM((slabs * nq, 32, 128), BF16),
            pltpu.VMEM((NH, 2, nq // 2, 32, 128), BF16),
            pltpu.VMEM((NH, 2, nq, 32, 128), BF16),
            pltpu.VMEM((NH * nq, 32, 128), BF16),
            pltpu.VMEM((NH * nq, 32, 128), BF16),
            pltpu.VMEM((2, 64, block), BF16),
            pltpu.VMEM((64, block), BF16),
            dma((12,)),
            dma((4,)),
            dma((4,)),
            dma((3,)),
            dma((3,)),
        ]
        + [dma((nz - 1,))] * 8
        + [dma((steps, nz, 2))] * 2
        + [dma((steps, 2))] * 6
        + [dma((ny + nz,))] * 2
        + [dma((2,))] * 5
        + [dma((2, 4))] * 2
        + [dma((2, 6))] * 2,
        compiler_params=pltpu.CompilerParams(
            collective_id=0, has_side_effects=True, vmem_limit_bytes=58 * 1024 * 1024
        ),
        cost_estimate=pl.CostEstimate(flops=2_700_000_000, bytes_accessed=8_000_000, transcendentals=131072),
    )(*args)
```

profile of v0, /device:TPU:1, one launch (start us, length us, event | category | flops | bytes accessed | tf_op | source)
XLA Modules:
  0.0 124.0 jit_solution(18334030898967729095)
XLA Ops:
  0.6 119.6 %shard_map.112 = (bf16[64,2048]{1,0:T(8,128)(2,1)}, f32[8,32,512]{2,1,0:T(8,128)}, f32[8,32,512]{2,1,0:T(8,128)}) custom-call(bf16[64,2048]{1,0:T(8,128)(2,1)} %refs_0_.1, s32[64,512]{1,0:T(8,128)} %refs_1_.1, s32[4,64]{1,0:T(4,128)} %bitcast.3, bf16[64,512]{1,0:T(8,128)(2,1)} %refs_3_.1, s32[2,16,1024]{2,1,0:T(8,128)} %refs_4_.1, s32[2,8,16]{2,1,0:T(8,128)} %bitcast.2, ...), custom_call_target="tpu_custom_call" | custom-call | flops 2700000000 | bytes 8000000 | tf_op jit(solution)/shard_map/pallas_call | solution.py:646
  120.2 0.0 copy-start.1
  120.2 1.7 %copy.15 = bf16[64,2048]{1,0:T(8,128)(2,1)} copy(bf16[64,2048]{1,0:T(8,128)(2,1)} %get-tuple-element.6) | data formatting | bytes 524288
  122.0 0.0 copy-done.1
  122.0 0.0 copy-start
  122.0 0.8 copy.16
  122.8 0.4 copy-done
  123.2 0.8 copy.17
Async XLA Ops:
  120.2 1.7 %copy-start.1 = (f32[8,32,512]{2,1,0:T(8,128)S(1)}, f32[8,32,512]{2,1,0:T(8,128)}, u32[]{:S(2)}) copy-start(f32[8,32,512]{2,1,0:T(8,128)} %get-tuple-element.7) | copy-start | bytes 1572868
  122.0 1.2 copy-start
where the time goes:
time: 125 us; the launch traced here: 124 us
  Pallas kernels  120 us (96%)
  local copies, waits for them, and re-layouts  3.75 us (3%)
    pallas_call x1, Pallas kernels, body(): pl.pallas_call(functools.partial(kernel, nz, ny), out_shape=(jax.ShapeDty...  120 us
    unnamed x7, local copies, waits for them, and re-layouts  3.75 us

commit v1 on v0

--- a/solution.py
+++ b/solution.py
@@ -29,8 +29,8 @@
 
 def kernel(nz, ny, *refs):
     inputs, refs = refs[:9], refs[9:]
-    outputs, fetched, held, refs = refs[:3], refs[3:12], refs[12:15], refs[15:]
-    update, new_first, new_second = held
+    outputs, fetched, held, refs = refs[:3], refs[3:12], refs[12:14], refs[14:]
+    update, (new_first, new_second) = outputs[0], held
     grad, lcodes, lscales, lerror, rcodes, rscales, rerror, first, second = fetched
     (
         turned,
@@ -48,12 +48,13 @@
         home,
         back,
         result,
-        foreign,
-    ) = refs[:16]
+    ) = refs[:15]
     (
         fetch_sem,
         sib_s,
         sib_r,
+        swap_s,
+        swap_r,
         grad_s,
         grad_r,
         zr_s,
@@ -83,7 +84,7 @@
         ring_r,
         sum_s,
         sum_r,
-    ) = refs[16:]
+    ) = refs[15:]
     nq = nz * ny
     block = 32 * nq
     order = 128 * nq
@@ -294,45 +295,46 @@
         next_b(b_step)
         b_step += 1
     landed(za)
+    start(ya[0])
     share(rows_a(y))
     for at in range(nz):
         landed(yr[last - 1][at])
 
     landed(rows_out)
+    lands = slabs.at[pl.ds(narrow * nq + place - odd, 2)]
+    high_far = 1 - high
+    n_far = x * NH + high_far
+    first_to = (nq // 2) * (2 * core + odd)
+
     wide_n = min(256, hb)
+    some = wide_n // 32
+
+    def send_near(begin, t, carry):
+        j = begin + lax.rem(2 * y + pair + t, some)
+        to = first_to + j
+
+        @pl.when(to != wide)
+        def _():
+            copy(outgoing.at[j], lands, out_s.at[0], out_r.at[0], to, narrow).start()
+
+        @pl.when(to == wide)
+        def _():
+            pltpu.make_async_copy(outgoing.at[j], lands, own_sem.at[0]).start()
+
+        return carry
+
+    def send_far(t, carry):
+        j = lax.rem(2 * y + pair + t, nq // 2)
+        copy(outgoing.at[j], lands, out_s.at[1], out_r.at[1], first_to + j, n_far).start()
+        return carry
+
     for at in range(0, hb, wide_n):
         basis = right[odd, :, :, :, at : at + wide_n].reshape(block, wide_n)
         value = jnp.dot(turned[...], basis, preferred_element_type=F32).T.astype(BF16)
         for d in range(2):
-            outgoing[at // 32 : (at + wide_n) // 32, d] = value[:, d * 128 : (d + 1) * 128].reshape(wide_n // 32, 32, 128)
-
-    lands = slabs.at[pl.ds(narrow * nq + place - odd, 2)]
-    high_far = 1 - high
-    n_far = x * NH + high_far
-    first_to = (nq // 2) * (2 * core + odd)
-
-    def send_near(t, carry):
-        j = lax.rem(2 * y + pair + t, nq // 2)
-        to = first_to + j
-
-        @pl.when(to != wide)
-        def _():
-            copy(outgoing.at[j], lands, out_s.at[0], out_r.at[0], to, narrow).start()
-
-        @pl.when(to == wide)
-        def _():
-            pltpu.make_async_copy(outgoing.at[j], lands, own_sem.at[0]).start()
-
-        return carry
-
-    def send_far(t, carry):
-        j = lax.rem(2 * y + pair + t, nq // 2)
-        copy(outgoing.at[j], lands, out_s.at[1], out_r.at[1], first_to + j, n_far).start()
-        return carry
-
-    lax.fori_loop(0, nq // 2, send_near, 0)
+            outgoing[at // 32 : at // 32 + some, d] = value[:, d * 128 : (d + 1) * 128].reshape(some, 32, 128)
+        lax.fori_loop(0, some, functools.partial(send_near, at // 32), 0)
     lax.fori_loop(0, nq // 2, send_far, 0)
-    start(ya[0])
 
     def wait_near(ref, base, send, recv, sending, some_own=has_own, own_many=1):
         def wait(many):
@@ -374,39 +376,46 @@
         return (xx * NH + g) * nq
 
     def ring_x(g, at):
-        own = slabs.at[pl.ds(slab_at(x, g), nq)]
+        own = [slabs.at[pl.ds(slab_at(x, g) + h * hq, hq)] for h in range(2)]
         from_down = slabs.at[pl.ds(slab_at(x_down, g), hq)]
         from_up = slabs.at[pl.ds(slab_at(x_up, g) + hq, hq)]
-        return [
-            copy(own, own, ring_s.at[at, 0], ring_r.at[at, 0], wide, n_up),
-            copy(own, own, ring_s.at[at, 1], ring_r.at[at, 1], wide, n_down),
-            copy(from_down, from_down, ring_s.at[at, 2], ring_r.at[at, 2], wide, n_up),
-            copy(from_up, from_up, ring_s.at[at, 3], ring_r.at[at, 3], wide, n_down),
+        made = [
+            (own[0], n_up),
+            (own[1], n_down),
+            (own[1], n_up),
+            (own[0], n_down),
+            (from_down, n_up),
+            (from_up, n_down),
         ]
+        return [copy(a, a, ring_s.at[at, i], ring_r.at[at, i], wide, nn) for i, (a, nn) in enumerate(made)]
 
     ring_near, ring_far = ring_x(high, 0), ring_x(high_far, 1)
+    next_a(1)
     wait_near(slabs, slab_at(x, high), out_s.at[0], out_r.at[0], False, sends_own, 2)
 
     @pl.when(sends_own)
     def _():
         pltpu.make_async_copy(outgoing.at[0], lands, own_sem.at[0]).wait()
 
-    start(ring_near[:2])
-    for t in range(1, last + 1):
+    start(ring_near[:4])
+    if last > 1:
+        next_a(2)
+    landed(ring_near[:2])
+    start(ring_near[4:])
+    if last > 2:
+        next_a(3)
+    wait_far(slabs, slab_at(x, high_far), out_s.at[1], out_r.at[1], False)
+    start(ring_far[:4])
+    for t in range(4, last + 1):
         next_a(t)
-        if t == last - 2 or (last == 2 and t == 1):
-            landed(ring_near[:2])
-            start(ring_near[2:])
-            wait_far(slabs, slab_at(x, high_far), out_s.at[1], out_r.at[1], False)
-            start(ring_far[:2])
-    landed(zlate)
-    start(late[0])
     landed(zb)
     for d in range(1, nz):
         zz = lax.rem(z + nz - d, nz)
         share(left.at[core, zz // 2, pl.ds(0, ny), lax.rem(zz, 2), pl.ds(ra, rb)])
     landed(ring_far[:2])
-    start(ring_far[2:])
+    start(ring_far[4:])
+    landed(zlate)
+    start(late[0])
     landed(ring_near[2:])
     landed(shares)
     landed(ring_far[2:])
@@ -450,9 +459,9 @@
         return carry
 
     lax.fori_loop(0, NX * NH, moments, 0)
-    stores = [pltpu.make_async_copy(held[i], outputs[i], fetch_sem.at[9 + i]) for i in range(3)]
-    stores[1].start()
-    stores[2].start()
+    stores = [pltpu.make_async_copy(held[i], outputs[1 + i], fetch_sem.at[9 + i]) for i in range(2)]
+    for c in stores:
+        c.start()
 
     def rotate_back(i, carry):
         at = i * 2
@@ -567,6 +576,7 @@
 
     turned_back = (back[0:nq].astype(F32) + back[nq : 2 * nq].astype(F32)).astype(BF16).reshape(block, 128)
     tall = ny * 32
+    swaps = []
     for zz in range(nz):
         value = sum(
             jnp.dot(
@@ -575,27 +585,19 @@
             for h in range(2)
         )
         value = value.T.astype(BF16)
-        result[0, :, zz * tall : (zz + 1) * tall] = value[0:64]
-        result[1, :, zz * tall : (zz + 1) * tall] = value[64:128]
-    swap = copy(result.at[other], foreign, sib_s.at[3], sib_r.at[3], sibling, narrow)
-    swap.start()
-    for h in range(2):
-
-        @pl.when(core == h)
-        def _():
-            update[:, h * block : (h + 1) * block] = result[core]
-
-    swap.wait_recv()
-    for h in range(2):
-
-        @pl.when(core != h)
-        def _():
-            update[:, h * block : (h + 1) * block] = foreign[...]
-
-    stores[0].start()
+        result[zz, 0] = value[0:64]
+        result[zz, 1] = value[64:128]
+        there = update.at[:, pl.ds(pl.multiple_of(core * block + zz * tall, tall), tall)]
+        swap = copy(result.at[zz, other], there, swap_s.at[zz], swap_r.at[zz], sibling, narrow)
+        swap.start()
+        swaps.append(swap)
+        store = pltpu.make_async_copy(result.at[zz, core], there, fetch_sem.at[11 + zz])
+        store.start()
+        stores.append(store)
+    landed(swaps)
 
     sent = sib + rows_out + zr + zlate + za + zb + [c for step in yr for part in step for c in part]
-    sent += [c for part in ya + yb + late for c in part] + shares + ring_near + ring_far + sums_near + sums_far + [swap]
+    sent += [c for part in ya + yb + late for c in part] + shares + ring_near + ring_far + sums_near + sums_far + swaps
     for c in sent:
         c.wait_send()
     for c in stores:
@@ -652,7 +654,7 @@
         ),
         in_specs=[anywhere] * 9,
         out_specs=(anywhere,) * 3,
-        scratch_shapes=[pltpu.VMEM(a.shape, a.dtype) for a in args + [args[0], args[7], args[8]]]
+        scratch_shapes=[pltpu.VMEM(a.shape, a.dtype) for a in args + args[7:9]]
         + [
             pltpu.VMEM((256, block), BF16),
             pltpu.VMEM((2, nz, ny, 32, block // 2), BF16),
@@ -668,11 +670,12 @@
             pltpu.VMEM((NH, 2, nq, 32, 128), BF16),
             pltpu.VMEM((NH * nq, 32, 128), BF16),
             pltpu.VMEM((NH * nq, 32, 128), BF16),
-            pltpu.VMEM((2, 64, block), BF16),
-            pltpu.VMEM((64, block), BF16),
-            dma((12,)),
-            dma((4,)),
-            dma((4,)),
+            pltpu.VMEM((nz, 2, 64, ny * 32), BF16),
+            dma((11 + nz,)),
+            dma((2,)),
+            dma((2,)),
+            dma((nz,)),
+            dma((nz,)),
             dma((3,)),
             dma((3,)),
         ]
@@ -681,8 +684,7 @@
         + [dma((steps, 2))] * 6
         + [dma((ny + nz,))] * 2
         + [dma((2,))] * 5
-        + [dma((2, 4))] * 2
-        + [dma((2, 6))] * 2,
+        + [dma((2, 6))] * 4,
         compiler_params=pltpu.CompilerParams(
             collective_id=0, has_side_effects=True, vmem_limit_bytes=58 * 1024 * 1024
         ),

time: 125 us -> 121 us (0.968)
  Pallas kernels: 120 us -> 116 us
    pallas_call x1, Pallas kernels: 120 us -> 116 us  [body(): pl.pallas_call(functools.partial(kernel, nz, ny), out_shape=(jax.ShapeDty...]
where the time goes in v1:
time: 121 us
  Pallas kernels  116 us (96%)
  local copies, waits for them, and re-layouts  3.75 us (3%)
    pallas_call x1, Pallas kernels, body(): pl.pallas_call(functools.partial(kernel, nz, ny), out_shape=(jax.ShapeDty...  116 us
    unnamed x7, local copies, waits for them, and re-layouts  3.75 us

profile of v1, /device:TPU:1, one launch (start us, length us, event | category | flops | bytes accessed | tf_op | source)
XLA Modules:
  0.0 120.6 jit_solution(16078350567415318909)
XLA Ops:
  0.6 116.2 %shard_map.112 = (bf16[64,2048]{1,0:T(8,128)(2,1)}, f32[8,32,512]{2,1,0:T(8,128)}, f32[8,32,512]{2,1,0:T(8,128)}) custom-call(bf16[64,2048]{1,0:T(8,128)(2,1)} %refs_0_.1, s32[64,512]{1,0:T(8,128)} %refs_1_.1, s32[4,64]{1,0:T(4,128)} %bitcast.3, bf16[64,512]{1,0:T(8,128)(2,1)} %refs_3_.1, s32[2,16,1024]{2,1,0:T(8,128)} %refs_4_.1, s32[2,8,16]{2,1,0:T(8,128)} %bitcast.2, ...), custom_call_target="tpu_custom_call" | custom-call | flops 2700000000 | bytes 8000000 | tf_op jit(solution)/shard_map/pallas_call | solution.py:648
  116.8 0.0 copy-start.1
  116.8 1.7 %copy.15 = bf16[64,2048]{1,0:T(8,128)(2,1)} copy(bf16[64,2048]{1,0:T(8,128)(2,1)} %get-tuple-element.6) | data formatting | bytes 524288
  118.5 0.0 copy-done.1
  118.5 0.0 copy-start
  118.5 0.8 copy.16
  119.3 0.4 copy-done
  119.8 0.8 copy.17
Async XLA Ops:
  116.8 1.7 %copy-start.1 = (f32[8,32,512]{2,1,0:T(8,128)S(1)}, f32[8,32,512]{2,1,0:T(8,128)}, u32[]{:S(2)}) copy-start(f32[8,32,512]{2,1,0:T(8,128)} %get-tuple-element.7) | copy-start | bytes 1572868
  118.5 1.2 %copy-start = (f32[8,32,512]{2,1,0:T(8,128)S(1)}, f32[8,32,512]{2,1,0:T(8,128)}, u32[]{:S(2)}) copy-start(f32[8,32,512]{2,1,0:T(8,128)} %get-tuple-element.8) | copy-start | bytes 1572868

commit v2 on v1

--- a/solution.py
+++ b/solution.py
@@ -168,23 +168,6 @@
         copy(own_block, turned.at[rows_g, :], grad_s.at[1], grad_r.at[1], beside, narrow),
         copy(other_block, turned.at[rows_g, :], grad_s.at[2], grad_r.at[2], beside + 1 - 2 * core, narrow),
     ]
-    sib[0].start()
-    quantum = 1.0 / (16.0 * math.sqrt(order))
-    for i in (1, 2, 3):
-        fetches[i].wait()
-    value = dequantized(lcodes[...], lscales[...], lerror[...], quantum)
-    for h in range(2):
-
-        @pl.when(core == h)
-        def _():
-            left[h, pair, y, odd, rows64, :] = value[:, h * half : (h + 1) * half]
-
-        @pl.when(core != h)
-        def _():
-            lstage[...] = value[:, h * half : (h + 1) * half]
-
-    sib[1].start()
-
     last = ny // 2
 
     def along_z(ref_for, send, recv):
@@ -200,8 +183,42 @@
     nearest = [0, 1, nz - 1][: min(nz, 3)] + list(range(2, nz - 1))
     if nz == 2:
         nearest = [0, 1]
-    zr = along_z(lambda zz: right.at[lax.rem(zz, 2), z, y], zr_s, zr_r)
-    zlate = along_z(lambda zz: right.at[1 - lax.rem(zz, 2), z, y], zl_s, zl_r)
+    def rows_to_line(which, send, recv):
+        made = []
+        for d in range(1, nz):
+            zz = lax.rem(z + d, nz)
+            h = lax.rem(zz + which, 2)
+            dst = right.at[h, z, y, rows16, :]
+            both = ((dst, core), (rstage.at[h], other))
+            made.append(
+                [
+                    copy(src, dst, send.at[d - 1, i], recv.at[d - 1, i], wide_at(zz, y, cc), narrow)
+                    for i, (src, cc) in enumerate(both)
+                ]
+            )
+        return made
+
+    zr = rows_to_line(0, zr_s, zr_r)
+    zlate = rows_to_line(1, zl_s, zl_r)
+
+    sib[0].start()
+    for e in nearest[1:]:
+        start(zr[e - 1])
+    quantum = 1.0 / (16.0 * math.sqrt(order))
+    for i in (1, 2, 3):
+        fetches[i].wait()
+    value = dequantized(lcodes[...], lscales[...], lerror[...], quantum)
+    for h in range(2):
+
+        @pl.when(core == h)
+        def _():
+            left[h, pair, y, odd, rows64, :] = value[:, h * half : (h + 1) * half]
+
+        @pl.when(core != h)
+        def _():
+            lstage[...] = value[:, h * half : (h + 1) * half]
+
+    sib[1].start()
 
     def ring_right(t, e):
         zz = lax.rem(z + nz - e, nz)
@@ -257,7 +274,6 @@
 
     sib[0].wait_recv()
     start(yr[0][0])
-    start(zr)
     fetches[0].wait()
     for h in range(2):
 
@@ -271,9 +287,10 @@
     start(za)
     for at, e in enumerate(nearest):
         if at > 0:
-            zr[e - 1].wait_recv()
+            landed(zr[e - 1])
             start(yr[0][at])
-    start(zlate)
+    for part in zlate:
+        start(part)
     b_step = 1
 
     def next_b(t):
@@ -414,7 +431,8 @@
         share(left.at[core, zz // 2, pl.ds(0, ny), lax.rem(zz, 2), pl.ds(ra, rb)])
     landed(ring_far[:2])
     start(ring_far[4:])
-    landed(zlate)
+    for part in zlate:
+        landed(part)
     start(late[0])
     landed(ring_near[2:])
     landed(shares)
@@ -444,7 +462,6 @@
             start(late[t])
 
     lax.fori_loop(0, nq // deep, rotate, 0)
-    next_late(1)
     fetches[7].wait()
     fetches[8].wait()
 
@@ -522,17 +539,19 @@
     lax.fori_loop(0, nq // 4, rotate_back, 0)
     start((sums_far[0], sums_far[2]))
     lax.fori_loop(nq // 4, nq // 2, rotate_back, 0)
-    next_late(2)
     start((sums_far[1], sums_far[3]))
     start(sums_near[:2])
+    next_late(1)
     landed(sums_far[:2])
     pass_on(high_far, 0)
     start(sums_far[4:])
     start(sums_near[2:4])
+    if last > 1:
+        next_late(2)
     landed(sums_near[:2])
     pass_on(high, 1)
     start(sums_near[4:])
-    for t in range(3, last + 1):
+    for t in range(3, last):
         next_late(t)
 
     goes_to = high * nq + lax.rem(wide, nq)
@@ -567,6 +586,8 @@
     landed(sums_near[2:])
     add_up(high, 1)
     lax.fori_loop(0, nq, back_near, 0)
+    if last > 2:
+        next_late(last)
     wait_far(back, high_far * nq, back_s.at[1], back_r.at[1], False)
     wait_near(back, high * nq, back_s.at[0], back_r.at[0], False)
 
@@ -596,7 +617,7 @@
         stores.append(store)
     landed(swaps)
 
-    sent = sib + rows_out + zr + zlate + za + zb + [c for step in yr for part in step for c in part]
+    sent = sib + rows_out + za + zb + [c for part in zr + zlate for c in part] + [c for step in yr for part in step for c in part]
     sent += [c for part in ya + yb + late for c in part] + shares + ring_near + ring_far + sums_near + sums_far + swaps
     for c in sent:
         c.wait_send()
@@ -679,7 +700,8 @@
             dma((3,)),
             dma((3,)),
         ]
-        + [dma((nz - 1,))] * 8
+        + [dma((nz - 1, 2))] * 4
+        + [dma((nz - 1,))] * 4
         + [dma((steps, nz, 2))] * 2
         + [dma((steps, 2))] * 6
         + [dma((ny + nz,))] * 2

time: 121 us -> 120 us (level)
  no operation moved by 1% of the time
where the time goes in v2:
time: 120 us
  Pallas kernels  116 us (97%)
  local copies, waits for them, and re-layouts  3.75 us (3%)
    pallas_call x1, Pallas kernels, body(): pl.pallas_call(functools.partial(kernel, nz, ny), out_shape=(jax.ShapeDty...  116 us
    unnamed x7, local copies, waits for them, and re-layouts  3.75 us

profile of v2, /device:TPU:1, one launch (start us, length us, event | category | flops | bytes accessed | tf_op | source)
XLA Modules:
  0.0 120.1 jit_solution(5070508343237414061)
XLA Ops:
  0.6 115.7 %shard_map.112 = (bf16[64,2048]{1,0:T(8,128)(2,1)}, f32[8,32,512]{2,1,0:T(8,128)}, f32[8,32,512]{2,1,0:T(8,128)}) custom-call(bf16[64,2048]{1,0:T(8,128)(2,1)} %refs_0_.1, s32[64,512]{1,0:T(8,128)} %refs_1_.1, s32[4,64]{1,0:T(4,128)} %bitcast.3, bf16[64,512]{1,0:T(8,128)(2,1)} %refs_3_.1, s32[2,16,1024]{2,1,0:T(8,128)} %refs_4_.1, s32[2,8,16]{2,1,0:T(8,128)} %bitcast.2, ...), custom_call_target="tpu_custom_call" | custom-call | flops 2700000000 | bytes 8000000 | tf_op jit(solution)/shard_map/pallas_call | solution.py:669
  116.4 0.0 copy-start.1
  116.4 1.7 %copy.15 = bf16[64,2048]{1,0:T(8,128)(2,1)} copy(bf16[64,2048]{1,0:T(8,128)(2,1)} %get-tuple-element.6) | data formatting | bytes 524288
  118.1 0.0 copy-done.1
  118.1 0.0 copy-start
  118.1 0.8 copy.16
  118.9 0.4 copy-done
  119.3 0.8 copy.17
Async XLA Ops:
  116.4 1.7 %copy-start.1 = (f32[8,32,512]{2,1,0:T(8,128)S(1)}, f32[8,32,512]{2,1,0:T(8,128)}, u32[]{:S(2)}) copy-start(f32[8,32,512]{2,1,0:T(8,128)} %get-tuple-element.7) | copy-start | bytes 1572868
  118.1 1.2 %copy-start = (f32[8,32,512]{2,1,0:T(8,128)S(1)}, f32[8,32,512]{2,1,0:T(8,128)}, u32[]{:S(2)}) copy-start(f32[8,32,512]{2,1,0:T(8,128)} %get-tuple-element.8) | copy-start | bytes 1572868

commit v3 on v2

--- a/solution.py
+++ b/solution.py
@@ -97,10 +97,11 @@
     x, high = narrow // NH, lax.rem(narrow, NH)
     other = 1 - core
     pair, odd = z // 2, lax.rem(z, 2)
+    mine_half = 1 - odd
     place = (pair * ny + y) * 2 + odd
     side = wide // nq
     has_own = side == core
-    sends_own = wide // (nq // 2) == 2 * core + odd
+    sends_own = wide // (nq // 2) == 2 * core + mine_half
 
     fetches = [pltpu.make_async_copy(a, b, fetch_sem.at[i]) for i, (a, b) in enumerate(zip(inputs, fetched))]
     for i in (4, 5, 6, 1, 2, 3, 0, 7, 8):
@@ -198,8 +199,8 @@
             )
         return made
 
-    zr = rows_to_line(0, zr_s, zr_r)
-    zlate = rows_to_line(1, zl_s, zl_r)
+    zr = rows_to_line(1, zr_s, zr_r)
+    zlate = rows_to_line(0, zl_s, zl_r)
 
     sib[0].start()
     for e in nearest[1:]:
@@ -226,7 +227,7 @@
         made = []
         for way, (yy, ww) in enumerate(zip(passed(t), (w_up, w_down))):
             if t < last or (at < nz // 2) == (way == 0):
-                ref = right.at[odd, zz, yy]
+                ref = right.at[mine_half, zz, yy]
                 made.append(copy(ref, ref, yr_s.at[t - 1, e, way], yr_r.at[t - 1, e, way], ww, narrow))
         return made
 
@@ -262,7 +263,7 @@
         a, b = (rows_b(up), rows_b(down)) if t < last else (rows_b(up, 0, rb // 2), rows_b(down, rb // 2, rb // 2))
         yb.append(both_ways(t, a, b, yb_s, yb_r))
         zs = (pl.ds(0, nz), pl.ds(0, nz)) if t < last else (pl.ds(0, nz // 2), pl.ds(nz // 2, nz // 2))
-        a, b = right.at[1 - odd, zs[0], up], right.at[1 - odd, zs[1], down]
+        a, b = right.at[odd, zs[0], up], right.at[odd, zs[1], down]
         late.append(both_ways(t, a, b, late_s, late_r))
     shares = []
 
@@ -321,7 +322,7 @@
     lands = slabs.at[pl.ds(narrow * nq + place - odd, 2)]
     high_far = 1 - high
     n_far = x * NH + high_far
-    first_to = (nq // 2) * (2 * core + odd)
+    first_to = (nq // 2) * (2 * core + mine_half)
 
     wide_n = min(256, hb)
     some = wide_n // 32
@@ -346,7 +347,7 @@
         return carry
 
     for at in range(0, hb, wide_n):
-        basis = right[odd, :, :, :, at : at + wide_n].reshape(block, wide_n)
+        basis = right[mine_half, :, :, :, at : at + wide_n].reshape(block, wide_n)
         value = jnp.dot(turned[...], basis, preferred_element_type=F32).T.astype(BF16)
         for d in range(2):
             outgoing[at // 32 : at // 32 + some, d] = value[:, d * 128 : (d + 1) * 128].reshape(some, 32, 128)
@@ -417,10 +418,10 @@
     start(ring_near[:4])
     if last > 1:
         next_a(2)
+    if last > 2:
+        next_a(3)
     landed(ring_near[:2])
     start(ring_near[4:])
-    if last > 2:
-        next_a(3)
     wait_far(slabs, slab_at(x, high_far), out_s.at[1], out_r.at[1], False)
     start(ring_far[:4])
     for t in range(4, last + 1):

time: 120 us -> 121 us (level)
  no operation moved by 1% of the time
where the time goes in v3:
time: 121 us
  Pallas kernels  117 us (97%)
  local copies, waits for them, and re-layouts  3.75 us (3%)
    pallas_call x1, Pallas kernels, body(): pl.pallas_call(functools.partial(kernel, nz, ny), out_shape=(jax.ShapeDty...  117 us
    unnamed x7, local copies, waits for them, and re-layouts  3.75 us

profile of v3, /device:TPU:1, one launch (start us, length us, event | category | flops | bytes accessed | tf_op | source)
XLA Modules:
  0.0 121.2 jit_solution(14011723846484071598)
XLA Ops:
  0.6 116.8 %shard_map.112 = (bf16[64,2048]{1,0:T(8,128)(2,1)}, f32[8,32,512]{2,1,0:T(8,128)}, f32[8,32,512]{2,1,0:T(8,128)}) custom-call(bf16[64,2048]{1,0:T(8,128)(2,1)} %refs_0_.1, s32[64,512]{1,0:T(8,128)} %refs_1_.1, s32[4,64]{1,0:T(4,128)} %bitcast.3, bf16[64,512]{1,0:T(8,128)(2,1)} %refs_3_.1, s32[2,16,1024]{2,1,0:T(8,128)} %refs_4_.1, s32[2,8,16]{2,1,0:T(8,128)} %bitcast.2, ...), custom_call_target="tpu_custom_call" | custom-call | flops 2700000000 | bytes 8000000 | tf_op jit(solution)/shard_map/pallas_call | solution.py:670
  117.4 0.0 copy-start.1
  117.4 1.7 %copy.15 = bf16[64,2048]{1,0:T(8,128)(2,1)} copy(bf16[64,2048]{1,0:T(8,128)(2,1)} %get-tuple-element.6) | data formatting | bytes 524288
  119.2 0.0 copy-done.1
  119.2 0.0 copy-start
  119.2 0.8 copy.16
  120.0 0.4 copy-done
  120.4 0.8 copy.17
Async XLA Ops:
  117.4 1.7 %copy-start.1 = (f32[8,32,512]{2,1,0:T(8,128)S(1)}, f32[8,32,512]{2,1,0:T(8,128)}, u32[]{:S(2)}) copy-start(f32[8,32,512]{2,1,0:T(8,128)} %get-tuple-element.7) | copy-start | bytes 1572868
  119.2 1.2 %copy-start = (f32[8,32,512]{2,1,0:T(8,128)S(1)}, f32[8,32,512]{2,1,0:T(8,128)}, u32[]{:S(2)}) copy-start(f32[8,32,512]{2,1,0:T(8,128)} %get-tuple-element.8) | copy-start | bytes 1572868

commit v4 on v2

--- a/solution.py
+++ b/solution.py
@@ -232,7 +232,7 @@
 
     yr = [[ring_right(t, e) for e in nearest] for t in range(1, last + 1)]
 
-    ra = 96
+    ra = 112
     rb = 128 - ra
 
     def rows_a(yy, zs=slice(None)):
@@ -259,8 +259,7 @@
         else:
             a, b = rows_a(up, pl.ds(0, 1)), rows_a(down, pl.ds(1, 1))
         ya.append(both_ways(t, a, b, ya_s, ya_r))
-        a, b = (rows_b(up), rows_b(down)) if t < last else (rows_b(up, 0, rb // 2), rows_b(down, rb // 2, rb // 2))
-        yb.append(both_ways(t, a, b, yb_s, yb_r))
+        yb.append(both_ways(t, rows_b(up), rows_b(down), yb_s, yb_r)[: 2 if t < last else 1])
         zs = (pl.ds(0, nz), pl.ds(0, nz)) if t < last else (pl.ds(0, nz // 2), pl.ds(nz // 2, nz // 2))
         a, b = right.at[1 - odd, zs[0], up], right.at[1 - odd, zs[1], down]
         late.append(both_ways(t, a, b, late_s, late_r))

time: 120 us -> 119 us (level)
  Pallas kernels: 116 us -> 114 us
    pallas_call x1, Pallas kernels: 116 us -> 114 us  [body(): pl.pallas_call(functools.partial(kernel, nz, ny), out_shape=(jax.ShapeDty...]
where the time goes in v4:
time: 119 us
  Pallas kernels  114 us (96%)
  local copies, waits for them, and re-layouts  3.75 us (3%)
    pallas_call x1, Pallas kernels, body(): pl.pallas_call(functools.partial(kernel, nz, ny), out_shape=(jax.ShapeDty...  114 us
    unnamed x7, local copies, waits for them, and re-layouts  3.75 us

profile of v4, /device:TPU:1, one launch (start us, length us, event | category | flops | bytes accessed | tf_op | source)
XLA Modules:
  0.0 118.8 jit_solution(7344307748741729255)
XLA Ops:
  0.6 114.4 %shard_map.112 = (bf16[64,2048]{1,0:T(8,128)(2,1)}, f32[8,32,512]{2,1,0:T(8,128)}, f32[8,32,512]{2,1,0:T(8,128)}) custom-call(bf16[64,2048]{1,0:T(8,128)(2,1)} %refs_0_.1, s32[64,512]{1,0:T(8,128)} %refs_1_.1, s32[4,64]{1,0:T(4,128)} %bitcast.3, bf16[64,512]{1,0:T(8,128)(2,1)} %refs_3_.1, s32[2,16,1024]{2,1,0:T(8,128)} %refs_4_.1, s32[2,8,16]{2,1,0:T(8,128)} %bitcast.2, ...), custom_call_target="tpu_custom_call" | custom-call | flops 2700000000 | bytes 8000000 | tf_op jit(solution)/shard_map/pallas_call | solution.py:668
  115.0 0.0 copy-start.1
  115.0 1.7 %copy.15 = bf16[64,2048]{1,0:T(8,128)(2,1)} copy(bf16[64,2048]{1,0:T(8,128)(2,1)} %get-tuple-element.6) | data formatting | bytes 524288
  116.8 0.0 copy-done.1
  116.8 0.0 copy-start
  116.8 0.8 copy.16
  117.6 0.4 copy-done
  118.0 0.8 copy.17
Async XLA Ops:
  115.0 1.7 %copy-start.1 = (f32[8,32,512]{2,1,0:T(8,128)S(1)}, f32[8,32,512]{2,1,0:T(8,128)}, u32[]{:S(2)}) copy-start(f32[8,32,512]{2,1,0:T(8,128)} %get-tuple-element.7) | copy-start | bytes 1572868
  116.8 1.2 %copy-start = (f32[8,32,512]{2,1,0:T(8,128)S(1)}, f32[8,32,512]{2,1,0:T(8,128)}, u32[]{:S(2)}) copy-start(f32[8,32,512]{2,1,0:T(8,128)} %get-tuple-element.8) | copy-start | bytes 1572868

commit v5 on v4

--- a/solution.py
+++ b/solution.py
@@ -322,6 +322,15 @@
     n_far = x * NH + high_far
     first_to = (nq // 2) * (2 * core + odd)
 
+    def next_a(t):
+        landed(ya[t - 1])
+        if t < last:
+            start(ya[t])
+            for yy in passed(t + 1):
+                share(rows_a(yy))
+        else:
+            share(rows_a(lax.rem(y + last, ny)))
+
     wide_n = min(256, hb)
     some = wide_n // 32
 
@@ -350,6 +359,8 @@
         for d in range(2):
             outgoing[at // 32 : at // 32 + some, d] = value[:, d * 128 : (d + 1) * 128].reshape(some, 32, 128)
         lax.fori_loop(0, some, functools.partial(send_near, at // 32), 0)
+        if at == 0:
+            next_a(1)
     lax.fori_loop(0, nq // 2, send_far, 0)
 
     def wait_near(ref, base, send, recv, sending, some_own=has_own, own_many=1):
@@ -376,15 +387,6 @@
             c.wait_send()
         else:
             c.wait_recv()
-
-    def next_a(t):
-        landed(ya[t - 1])
-        if t < last:
-            start(ya[t])
-            for yy in passed(t + 1):
-                share(rows_a(yy))
-        else:
-            share(rows_a(lax.rem(y + last, ny)))
 
     hq = nq // 2
 
@@ -406,7 +408,6 @@
         return [copy(a, a, ring_s.at[at, i], ring_r.at[at, i], wide, nn) for i, (a, nn) in enumerate(made)]
 
     ring_near, ring_far = ring_x(high, 0), ring_x(high_far, 1)
-    next_a(1)
     wait_near(slabs, slab_at(x, high), out_s.at[0], out_r.at[0], False, sends_own, 2)
 
     @pl.when(sends_own)
@@ -416,10 +417,10 @@
     start(ring_near[:4])
     if last > 1:
         next_a(2)
+    if last > 2:
+        next_a(3)
     landed(ring_near[:2])
     start(ring_near[4:])
-    if last > 2:
-        next_a(3)
     wait_far(slabs, slab_at(x, high_far), out_s.at[1], out_r.at[1], False)
     start(ring_far[:4])
     for t in range(4, last + 1):

time: 119 us -> 126 us (1.059)
  Pallas kernels: 114 us -> 121 us
    pallas_call x1, Pallas kernels: 114 us -> 121 us  [body(): pl.pallas_call(functools.partial(kernel, nz, ny), out_shape=(jax.ShapeDty...]
where the time goes in v5:
time: 126 us
  Pallas kernels  121 us (96%)
  local copies, waits for them, and re-layouts  3.75 us (3%)
    pallas_call x1, Pallas kernels, body(): pl.pallas_call(functools.partial(kernel, nz, ny), out_shape=(jax.ShapeDty...  121 us
    unnamed x7, local copies, waits for them, and re-layouts  3.75 us

profile of v5, /device:TPU:1, one launch (start us, length us, event | category | flops | bytes accessed | tf_op | source)
XLA Modules:
  0.0 125.6 jit_solution(1299531191526444163)
XLA Ops:
  0.6 121.2 %shard_map.112 = (bf16[64,2048]{1,0:T(8,128)(2,1)}, f32[8,32,512]{2,1,0:T(8,128)}, f32[8,32,512]{2,1,0:T(8,128)}) custom-call(bf16[64,2048]{1,0:T(8,128)(2,1)} %refs_0_.1, s32[64,512]{1,0:T(8,128)} %refs_1_.1, s32[4,64]{1,0:T(4,128)} %bitcast.3, bf16[64,512]{1,0:T(8,128)(2,1)} %refs_3_.1, s32[2,16,1024]{2,1,0:T(8,128)} %refs_4_.1, s32[2,8,16]{2,1,0:T(8,128)} %bitcast.2, ...), custom_call_target="tpu_custom_call" | custom-call | flops 2700000000 | bytes 8000000 | tf_op jit(solution)/shard_map/pallas_call | solution.py:669
  121.8 0.0 copy-start.1
  121.8 1.7 %copy.15 = bf16[64,2048]{1,0:T(8,128)(2,1)} copy(bf16[64,2048]{1,0:T(8,128)(2,1)} %get-tuple-element.6) | data formatting | bytes 524288
  123.5 0.0 copy-done.1
  123.6 0.0 copy-start
  123.6 0.8 copy.16
  124.3 0.4 copy-done
  124.8 0.8 copy.17
Async XLA Ops:
  121.8 1.7 %copy-start.1 = (f32[8,32,512]{2,1,0:T(8,128)S(1)}, f32[8,32,512]{2,1,0:T(8,128)}, u32[]{:S(2)}) copy-start(f32[8,32,512]{2,1,0:T(8,128)} %get-tuple-element.7) | copy-start | bytes 1572868
  123.6 1.2 copy-start
